TPU v7x, 256 devices: a whole 4x4x8 slice. The times are simulated.
256 devices in a mesh: dp: 32 (over y, x, z_hi), tensor: 8 (over z_lo, core).
Axes of the slice: x: 4, y: 4, z: 8 (z_hi: 2, z_lo: 4; z = z_hi * 4 + z_lo), core: 2. Of those that a mesh axis runs over, the one named last changes fastest.
Arguments:
- projected: bfloat16 [32, 512, 3, 5120], P('dp', 'tensor'), may hold values from -6 to 6
- projected_tan: bfloat16 [32, 512, 3, 5120], P('dp', 'tensor'), may hold values from -6 to 6
- hidden: bfloat16 [32, 512, 5120], P('dp', 'tensor'), may hold values from -6 to 6
- hidden_tan: bfloat16 [32, 512, 5120], P('dp', 'tensor'), may hold values from -6 to 6
- out_weight: bfloat16 [5120, 5120], P('tensor', 'dp'), may hold values from -0.078125 to 0.078125
- gate_table: float32 [32, 5120], replicated, may hold values from 0.5 to 1.5
- gate_rate: float32 [32, 5120], replicated, may hold values from -6 to 6
- timestep: int32 [32], P('dp'), may hold values from 0 to 31
Outputs:
- block_out: bfloat16 [32, 512, 5120], P('dp', 'tensor')
- block_tan: bfloat16 [32, 512, 5120], P('dp', 'tensor')
All inputs are finite; a program needn't handle non-finite values.
Results may differ from a plain program's by a relative error of at most 0.017.
Values may be sent and summed in bfloat16 or wider, within the bound.
A program may use at most 128 MiB of HBM per device.

v0:
```python
import math

import jax
import jax.numpy as jnp
from jax import lax
from jax.sharding import PartitionSpec as P

HEAD = 128


def attend_block(queries, query_tan, key_rows, value_rows, key_tan, value_tan):
    score_scale = 1.0 / math.sqrt(queries.shape[-1])
    scores = (
        jnp.einsum("qhd,khd->hqk", queries, key_rows, preferred_element_type=jnp.float32)
        * score_scale
    )
    probs = jax.nn.softmax(scores, axis=-1)
    probs_low = probs.astype(jnp.bfloat16)
    attended = jnp.einsum("hqk,khd->qhd", probs_low, value_rows, preferred_element_type=jnp.float32)
    first_part = jnp.einsum("qhd,khd->hqk", query_tan, key_rows, preferred_element_type=jnp.float32)
    second_part = jnp.einsum("qhd,khd->hqk", queries, key_tan, preferred_element_type=jnp.float32)
    scores_tan = (first_part + second_part) * score_scale
    probs_tan = probs * (scores_tan - jnp.sum(probs * scores_tan, axis=-1, keepdims=True))
    attended_tan = jnp.einsum(
        "hqk,khd->qhd",
        probs_tan.astype(jnp.bfloat16),
        value_rows,
        preferred_element_type=jnp.float32,
    )
    attended_tan = attended_tan + jnp.einsum(
        "hqk,khd->qhd", probs_low, value_tan, preferred_element_type=jnp.float32
    )
    return (attended.astype(jnp.bfloat16), attended_tan.astype(jnp.bfloat16))


def attend_clip(clip_items):
    packed, packed_tan = clip_items
    length = packed.shape[0]
    block_rows = min(length, 512)
    count_blocks = length // block_rows
    query_all, key_rows, value_rows = (packed[:, 0], packed[:, 1], packed[:, 2])
    query_tan_all, key_tan, value_tan = (packed_tan[:, 0], packed_tan[:, 1], packed_tan[:, 2])

    def one_block(block_start):
        return attend_block(query_all, query_tan_all, key_rows, value_rows, key_tan, value_tan)

    block_starts = jnp.arange(count_blocks, dtype=jnp.int32) * block_rows
    attended, attended_tan = lax.map(one_block, block_starts)
    return (attended.reshape(length, -1), attended_tan.reshape(length, -1))


def shards(
    projected, projected_tan, hidden, hidden_tan, out_weight, gate_table, gate_rate, timestep
):
    gathered, gathered_tan = (
        lax.all_to_all(projected, "tensor", split_axis=3, concat_axis=1, tiled=True),
        lax.all_to_all(projected_tan, "tensor", split_axis=3, concat_axis=1, tiled=True),
    )
    clip_count = gathered.shape[0]
    length = gathered.shape[1]
    local_heads = gathered.shape[3] // HEAD
    packed = gathered.reshape(clip_count, length, 3, local_heads, HEAD)
    packed_tan = gathered_tan.reshape(clip_count, length, 3, local_heads, HEAD)
    attended, attended_tan = lax.map(attend_clip, (packed, packed_tan))
    stacked = jnp.stack([attended, attended_tan], axis=0)
    full_weight = lax.all_gather(out_weight, "dp", axis=1, tiled=True)
    partial_terms = jnp.einsum(
        "bclh,hd->bcld", stacked, full_weight, preferred_element_type=jnp.float32
    )
    summed = lax.psum_scatter(
        partial_terms.astype(jnp.bfloat16), "tensor", scatter_dimension=2, tiled=True
    ).astype(jnp.float32)
    levels = gate_table.shape[0]
    onehot = (timestep[:, None] == jnp.arange(levels, dtype=jnp.int32)[None, :]).astype(jnp.float32)
    gate_rows = jnp.dot(onehot, gate_table, precision=lax.Precision.HIGHEST)[:, None, :]
    rate_rows = jnp.dot(onehot, gate_rate, precision=lax.Precision.HIGHEST)[:, None, :]
    block_out = (hidden.astype(jnp.float32) + gate_rows * summed[0]).astype(jnp.bfloat16)
    block_tan = (
        hidden_tan.astype(jnp.float32) + gate_rows * summed[1] + rate_rows * summed[0]
    ).astype(jnp.bfloat16)
    return (block_out, block_tan)


def solution(mesh):
    return jax.shard_map(
        shards,
        mesh=mesh,
        in_specs=(
            P("dp", "tensor", None, None),
            P("dp", "tensor", None, None),
            P("dp", "tensor", None),
            P("dp", "tensor", None),
            P("tensor", "dp"),
            P(),
            P(),
            P("dp"),
        ),
        out_specs=(P("dp", "tensor", None), P("dp", "tensor", None)),
        check_vma=False,
    )
```

profile of v0, /device:TPU:1, one launch (start us, length us, event | category | flops | bytes accessed | tf_op | source)
XLA Modules:
  0.0 360.8 jit_solution(155938103911554850)
XLA Ops:
  7.9 7.3 %copy.33 = bf16[1,64,3,5120]{1,2,0,3:T(4,128)(2,1)} copy(bf16[1,64,3,5120]{3,1,2,0:T(8,128)(2,1)} %param.8) | data formatting | bytes 3932160 | tf_op args[0]
  15.2 7.9 %reshape.153 = bf16[8,2,61440]{2,1,0:T(2,128)(2,1)} reshape(bf16[5120,1,3,64]{3,2,1,0:T(4,128)(2,1)} %bitcast.105) | data formatting | bytes 3932160
  23.1 7.4 %all-to-all-start = ((bf16[8,2,61440]{2,1,0:T(2,128)(2,1)}), bf16[8,2,61440]{2,1,0:T(2,128)(2,1)S(1)}, u32[]{:S(2)}, u32[]{:S(2)}) async-start(bf16[8,2,61440]{2,1,0:T(2,128)(2,1)} %reshape.153), calls=%async_computation | async-start | bytes 3932160 | tf_op jit(solution)/shard_map/all_to_all | solution.py:56
  30.5 7.3 %copy.39 = bf16[1,64,3,5120]{1,2,0,3:T(4,128)(2,1)} copy(bf16[1,64,3,5120]{3,1,2,0:T(8,128)(2,1)} %param.9) | data formatting | bytes 3932160 | tf_op args[1]
  37.8 7.9 %reshape.151 = bf16[8,2,61440]{2,1,0:T(2,128)(2,1)} reshape(bf16[5120,1,3,64]{3,2,1,0:T(4,128)(2,1)} %bitcast.106) | data formatting | bytes 3932160
  45.7 44.6 %all-to-all-done = bf16[8,2,61440]{2,1,0:T(2,128)(2,1)S(1)} async-done(((bf16[8,2,61440]{2,1,0:T(2,128)(2,1)}), bf16[8,2,61440]{2,1,0:T(2,128)(2,1)S(1)}, u32[]{:S(2)}, u32[]{:S(2)}) %all-to-all-start) | async-done | bytes 1966112 | tf_op jit(solution)/shard_map/all_to_all | solution.py:56
  90.3 4.7 %all-to-all-start.1 = ((bf16[8,2,61440]{2,1,0:T(2,128)(2,1)}), bf16[8,2,61440]{2,1,0:T(2,128)(2,1)}, u32[]{:S(2)}, u32[]{:S(2)}) async-start(bf16[8,2,61440]{2,1,0:T(2,128)(2,1)} %reshape.151), calls=%async_computation.1 | async-start | bytes 3932160 | tf_op jit(solution)/shard_map/all_to_all | solution.py:57
  94.9 5.3 %reshape.154 = bf16[5120,1,3,64]{3,2,1,0:T(4,128)(2,1)} reshape(bf16[8,2,61440]{2,1,0:T(2,128)(2,1)S(1)} %all-to-all-done) | data formatting | bytes 3932160
  100.3 5.9 %copy.34 = bf16[1,64,3,8,640]{4,1,3,2,0:T(8,128)(2,1)S(1)} copy(bf16[1,64,3,8,640]{1,2,4,3,0:T(4,128)(2,1)} %bitcast.103) | data formatting | bytes 3932160 | tf_op jit(solution)/shard_map/all_to_all | solution.py:56
  106.2 3.5 squeeze.40
  109.7 75.1 %all-to-all-done.1 = bf16[8,2,61440]{2,1,0:T(2,128)(2,1)} async-done(((bf16[8,2,61440]{2,1,0:T(2,128)(2,1)}), bf16[8,2,61440]{2,1,0:T(2,128)(2,1)}, u32[]{:S(2)}, u32[]{:S(2)}) %all-to-all-start.1) | async-done | bytes 1966112 | tf_op jit(solution)/shard_map/all_to_all | solution.py:57
  184.9 7.7 %reshape.152 = bf16[5120,1,3,64]{3,2,1,0:T(4,128)(2,1)} reshape(bf16[8,2,61440]{2,1,0:T(2,128)(2,1)} %all-to-all-done.1) | data formatting | bytes 3932160
  192.6 5.9 %copy.40 = bf16[1,64,3,8,640]{4,1,3,2,0:T(8,128)(2,1)S(1)} copy(bf16[1,64,3,8,640]{1,2,4,3,0:T(4,128)(2,1)} %bitcast.104) | data formatting | bytes 3932160 | tf_op jit(solution)/shard_map/all_to_all | solution.py:57
  198.5 3.5 squeeze.44
  202.0 5.5 %fusion.38 = (bf16[512,1,5,128]{3,2,0,1:T(8,128)(2,1)S(1)}, bf16[512,1,5,128]{3,2,0,1:T(8,128)(2,1)}, bf16[512,1,5,128]{3,2,0,1:T(8,128)(2,1)}, bf16[512,1,5,128...) fusion(bf16[512,3,5,128]{3,2,0,1:T(8,128)(2,1)} %squeeze.40, ...), kind=kLoop, calls=%fused_computation.52 | loop fusion | bytes 7864320 | tf_op jit(solution)/shard_map/while/body/eval_jaxpr/slice | solution.py:41
  207.5 1.3 copy.57
  209.4 5.9 %fusion.41 = (f32[5,512]{1,0:T(8,128)S(1)}, f32[5,512,512]{1,2,0:T(8,128)}) fusion(bf16[512,1,5,128]{3,2,0,1:T(8,128)(2,1)} %get-tuple-element.50, bf16[512,1,5,128]{3,2,0,1:T(8,128)(2,1)} %get-tuple-element.49), kind=kOutput, calls=%fused_computation.55 | convolution fusion | flops 339476992 | bytes 6563840 | tf_op jit(solution)/shard_map/while/body/eval_jaxpr/while/body/eval_jaxpr/sub | solution.py:17
  216.4 1.6 copy-done.9
  219.6 1.4 multiply_reduce_fusion
  222.3 3.0 convolution_convert_fusion
  225.6 14.1 %convert_bitcast_fusion = bf16[2,1,512,5120]{3,2,0,1:T(8,128)(2,1)} fusion(bf16[640,5120]{0,1:T(8,128)(2,1)} %all-gather.2.cloned.1.call-done, bf16[1,1,512,640]{3,2,0,1:T(8,128)(2,1)S(1)} %copy.47, bf16[1,1,512,640]{3,2,0,1:T(8,128)(2,1)S(1)} %copy.46), kind=kOutput, calls=%fused_computation.1 | convolution fusion | flops 6716784640 | bytes 18350080 | tf_op jit(solution)/shard_map/bclh,hd->bcld/dot_general | solution.py:67
  241.3 109.3 %reduce-scatter.2.cloned.1.call-done = bf16[2,1,64,5120]{3,2,0,1:T(8,128)(2,1)} async-done(((bf16[2,1,512,5120]{3,2,0,1:T(8,128)(2,1)}), bf16[2,1,64,5120]{3,2,0,1:T(8,128)(2,1)}) %reduce-scatter.2.cloned.1.call-update) | async-done | bytes 1310736 | tf_op jit(solution)/shard_map/reduce_scatter | solution.py:70
  350.5 1.9 fusion.40
  352.5 1.5 fusion.13
  (32 shorter events, 6.3 us)
Async XLA Ops:
  7.2 233.4 %copy-start = (f32[32,5120]{1,0:T(8,128)S(1)}, f32[32,5120]{1,0:T(8,128)}, u32[]{:S(2)}) copy-start(f32[32,5120]{1,0:T(8,128)} %param.13) | copy-start | bytes 1966084
  7.2 218.4 %all-gather.2.cloned.1.call-start = ((), (), s32[]{:S(2)}) async-start(), calls=%async_computation.3 | async-start | bytes 6758400 | tf_op jit(solution)/shard_map/all_gather | solution.py:66
  23.1 67.2 %all-to-all-start = ((bf16[8,2,61440]{2,1,0:T(2,128)(2,1)}), bf16[8,2,61440]{2,1,0:T(2,128)(2,1)S(1)}, u32[]{:S(2)}, u32[]{:S(2)}) async-start(bf16[8,2,61440]{2,1,0:T(2,128)(2,1)} %reshape.153), calls=%async_computation | async-start | bytes 3932160 | tf_op jit(solution)/shard_map/all_to_all | solution.py:56
  90.3 94.6 %all-to-all-start.1 = ((bf16[8,2,61440]{2,1,0:T(2,128)(2,1)}), bf16[8,2,61440]{2,1,0:T(2,128)(2,1)}, u32[]{:S(2)}, u32[]{:S(2)}) async-start(bf16[8,2,61440]{2,1,0:T(2,128)(2,1)} %reshape.151), calls=%async_computation.1 | async-start | bytes 3932160 | tf_op jit(solution)/shard_map/all_to_all | solution.py:57
  94.9 255.6 %reduce-scatter.2.cloned.1.call-start = ((), (), s32[]{:S(2)}) async-start(), calls=%async_computation.4 | async-start | bytes 11796480 | tf_op jit(solution)/shard_map/reduce_scatter | solution.py:70
  208.8 6.5 %copy-start.1 = (bf16[512,1,5,128]{3,2,0,1:T(8,128)(2,1)S(1)}, bf16[512,1,5,128]{3,2,0,1:T(8,128)(2,1)}, u32[]{:S(2)}) copy-start(bf16[512,1,5,128]{3,2,0,1:T(8,128)(2,1)} %get-tuple-element.49) | copy-start | bytes 1966084
  209.4 5.9 %copy-start.2 = (bf16[512,1,5,128]{3,2,0,1:T(8,128)(2,1)S(1)}, bf16[512,1,5,128]{3,2,0,1:T(8,128)(2,1)}, u32[]{:S(2)}) copy-start(bf16[512,1,5,128]{3,2,0,1:T(8,128)(2,1)} %get-tuple-element.68) | copy-start | bytes 1966084
  215.3 1.1 copy-start.8
  215.3 2.7 copy-start.9
  218.0 1.2 copy-start.3
  218.0 1.5 copy-start.4
  239.7 1.2 copy-start.7
  239.8 112.7 %copy-start.5 = (bf16[1,64,5120]{2,1,0:T(8,128)(2,1)S(1)}, bf16[1,64,5120]{2,1,0:T(8,128)(2,1)}, u32[]{:S(2)}) copy-start(bf16[1,64,5120]{2,1,0:T(8,128)(2,1)} %param.11) | copy-start | bytes 1966084
  239.8 112.7 %copy-start.6 = (bf16[1,64,5120]{2,1,0:T(8,128)(2,1)S(1)}, bf16[1,64,5120]{2,1,0:T(8,128)(2,1)}, u32[]{:S(2)}) copy-start(bf16[1,64,5120]{2,1,0:T(8,128)(2,1)} %param.10) | copy-start | bytes 1966084
Sparse Core Ops, SparseCore 0:
  11.4 152.7 all-gather.1
  239.9 110.6 reduce-scatter.1
where the time goes:
time: 364 us; the launch traced here: 361 us
  waiting for transfers between devices  230 us (63%)
  local copies, waits for them, and re-layouts  73 us (20%)
  matrix products  27.5 us (8%)
  between operations  15 us (4%)
  starting transfers between devices  12.1 us (3%)
    reduce_scatter x1, waiting for transfers between devices, shards(): lax.psum_scatter(partial_terms.astype(jnp.bfloat16), 'tensor', scatter_di...  109 us
    all_to_all x1, waiting for transfers between devices, shards(): lax.all_to_all(projected_tan, 'tensor', split_axis=3, concat_axis=1, tile...  75.1 us
    unnamed x28, local copies, waits for them, and re-layouts  48.1 us
    all_to_all x1, waiting for transfers between devices, shards(): lax.all_to_all(projected, 'tensor', split_axis=3, concat_axis=1, tiled=True)  44.6 us
    dot_general x1, matrix products, shards(): jnp.einsum('bclh,hd->bcld', stacked, full_weight, preferred_element_type=...  14.1 us
    all_to_all x1, starting transfers between devices, shards(): lax.all_to_all(projected, 'tensor', split_axis=3, concat_axis=1, tiled=True)  7.4 us
  transfers between devices with their start and end apart: 4, of which 3 were waited for; matrix products, arithmetic and copies ran while one was open for 23% of the time, Pallas kernels for 0%

commit v1 on v0

v1 whole, which is shorter than its diff:
```python
import math

import jax
import jax.numpy as jnp
from jax import lax
from jax.experimental import pallas as pl
from jax.experimental.pallas import tpu as pltpu
from jax.sharding import PartitionSpec as P

HEAD = 128
PARTS = 5
LEN = 512
ROWS = 64
NT = 8
SIDE = 4
RING = 8
COLS = 160
SLICE = 1280
TILES = 5
TILE = 256
D = 5120
AHEAD = 2
BLOCK = 256
PEER_ORDER = (6, 4, 7, 5, 2, 3, 1)
SCALE = 1.0 / math.sqrt(HEAD)
MESH = pl.DeviceIdType.MESH
NT_DIMS = (((1,), (1,)), ((), ()))


def place(y, x, z, core):
    return (y * 8 + x * 2 + z // SIDE, (z % SIDE) * 2 + core)


def aligned(value, size, base):
    return pl.ds(pl.multiple_of(value, base), size)


def kernel(
    proj, ptan, hidden, hidden_tan, weight, gate_table, gate_rate, timestep,
    out, out_tan,
    xbuf, att, tok, wbuf, acc, out_send, out_recv, hid, hid_tan, gates, rates,
    fwd_send, fwd_recv, back_send, back_recv, tok_send, tok_recv,
    z_send, z_recv, x_send, x_recv, core_send, core_recv, res_send, res_recv, local_sem, own_sem,
):
    dp, me = lax.axis_index("dp"), lax.axis_index("tensor")
    y, x, z_hi = dp // 8, (dp % 8) // 2, dp % 2
    z_lo, core = me // 2, me % 2
    z = z_hi * SIDE + z_lo
    lane = (core * SIDE + z_lo) * HEAD
    z_right = place(y, x, (z + 1) % RING, core)
    z_left = place(y, x, (z + RING - 1) % RING, core)
    x_peers = [place(y, (x + k) % SIDE, z, core) for k in range(1, SIDE)]
    y_peers = [place((y + k) % SIDE, x, z, core) for k in range(1, SIDE)]
    tensor_peers = [(me + k) % NT for k in range(1, NT)]
    sibling = (dp, z_lo * 2 + 1 - core)

    def remote(src, dst, send, recv, device):
        copy = pltpu.make_async_remote_copy(
            src_ref=src, dst_ref=dst, send_sem=send, recv_sem=recv, device_id=device, device_id_type=MESH
        )
        copy.start()
        return copy

    def wait_bytes(ref, sem):
        pltpu.make_async_copy(ref, ref, sem).wait()

    barrier = pltpu.get_barrier_semaphore()
    greeted = [(dp, peer) for peer in tensor_peers] + [z_right, z_left] + x_peers + y_peers
    for device in greeted:
        pl.semaphore_signal(barrier, inc=1, device_id=device, device_id_type=MESH)
    pl.semaphore_wait(barrier, len(greeted))

    def xor_peer(k):
        result = 0
        for bit in (1, 2, 4):
            mine = (me // bit) % 2
            result = result + bit * ((1 - mine) if k & bit else mine)
        return result

    peers = [xor_peer(k) for k in PEER_ORDER]
    mine_rows = aligned(ROWS * me, ROWS, ROWS)

    def start_forward(j):
        for peer in peers:
            columns = aligned((peer * PARTS + j) * HEAD, HEAD, HEAD)
            for half, source in enumerate((proj, ptan)):
                remote(
                    source.at[:, :, columns],
                    xbuf.at[j, pl.ds(3 * half, 3), mine_rows, :],
                    fwd_send.at[j],
                    fwd_recv.at[j],
                    (dp, peer),
                )
        columns = aligned((me * PARTS + j) * HEAD, HEAD, HEAD)
        for half, source in enumerate((proj, ptan)):
            pltpu.make_async_copy(
                source.at[:, :, columns], xbuf.at[j, pl.ds(3 * half, 3), mine_rows, :], fwd_recv.at[j]
            ).start()

    def start_back(j):
        lanes = aligned(lane, HEAD, HEAD)
        for peer in peers:
            remote(
                att.at[j, :, aligned(ROWS * peer, ROWS, ROWS), :],
                tok.at[j, y, :, :, lanes],
                back_send.at[j],
                back_recv.at[j],
                (dp, peer),
            )
        pltpu.make_async_copy(att.at[j, :, mine_rows, :], tok.at[j, y, :, :, lanes], back_recv.at[j]).start()

    def start_tokens(j):
        wait_bytes(tok.at[j, y], back_recv.at[j])
        for k, peer in enumerate(y_peers):
            remote(tok.at[j, y], tok.at[j, y], tok_send.at[j, k], tok_recv.at[j, k], peer)

    def wait_tokens(j):
        for k in range(SIDE - 1):
            wait_bytes(tok.at[j, (y + SIDE - 1 - k) % SIDE], tok_recv.at[j, k])

    def attend(j):
        def block(b, carry):
            rows = aligned(b * BLOCK, BLOCK, BLOCK)
            q, qt = xbuf[j, 0, rows, :], xbuf[j, 3, rows, :]
            k, v, kt, vt = xbuf[j, 1], xbuf[j, 2], xbuf[j, 4], xbuf[j, 5]
            s = lax.dot_general(q, k, NT_DIMS, preferred_element_type=jnp.float32)
            st = lax.dot_general(
                jnp.concatenate([qt, q], axis=1),
                jnp.concatenate([k, kt], axis=1),
                NT_DIMS,
                preferred_element_type=jnp.float32,
            )
            top = jnp.max(s, axis=-1, keepdims=True)
            e = jnp.exp2((s - top) * (SCALE * math.log2(math.e)))
            probs = e * (1.0 / jnp.sum(e, axis=-1, keepdims=True))
            low = probs.astype(jnp.bfloat16)
            mean = jnp.sum(probs * st, axis=-1, keepdims=True)
            probs_tan = (probs * ((st - mean) * SCALE)).astype(jnp.bfloat16)
            both = jnp.dot(low, jnp.concatenate([v, vt], axis=1), preferred_element_type=jnp.float32)
            tan = jnp.dot(probs_tan, v, preferred_element_type=jnp.float32) + both[:, HEAD:]
            att[j, 0, rows, :] = both[:, :HEAD].astype(jnp.bfloat16)
            att[j, 1, rows, :] = tan.astype(jnp.bfloat16)
            return carry

        lax.fori_loop(0, LEN // BLOCK, block, 0)

    def project(j):
        rows = tok[j].reshape(SIDE * 2 * ROWS, NT * HEAD)

        def tile(n, carry):
            part = lax.dot_general(
                rows,
                wbuf[j, aligned(n * TILE, TILE, TILE), :],
                NT_DIMS,
                preferred_element_type=jnp.float32,
            )
            if j == 0:
                acc[n] = part
            else:
                acc[n] = acc[n] + part
            return carry

        lax.fori_loop(0, TILES, tile, 0)

    def shard(which, parts=pl.ds(0, PARTS)):
        return wbuf.at[
            parts,
            aligned(x * 2 * COLS + (which // SIDE) * COLS, COLS, COLS),
            aligned((core * SIDE + which % SIDE) * HEAD, HEAD, HEAD),
        ]

    def slab(which_x, which_core):
        return wbuf.at[
            :, aligned(which_x * 2 * COLS, 2 * COLS, 2 * COLS), aligned(which_core * SIDE * HEAD, SIDE * HEAD, SIDE * HEAD)
        ]

    locals_ = []
    for j in range(PARTS):
        locals_.append(
            pltpu.make_async_copy(
                weight.at[:, pl.ds(j * HEAD, HEAD)],
                wbuf.at[j, aligned((x * 2 + z_hi) * COLS, COLS, COLS), aligned(lane, HEAD, HEAD)],
                own_sem.at[0],
            )
        )
    for copy in locals_:
        copy.start()
    wait_bytes(shard(z), own_sem.at[0])
    sends = []
    right_parts, left_parts = pl.ds(0, 3), pl.ds(3, 2)

    def ring_step(s):
        to_right, to_left = (z + RING - s) % RING, (z + s) % RING
        if s < 3:
            a, b = shard(to_right), shard(to_left)
        else:
            a, b = shard(to_right, right_parts), shard(to_left, left_parts)
        sends.append(remote(a, a, z_send.at[0, s], z_recv.at[0, s], z_right))
        sends.append(remote(b, b, z_send.at[1, s], z_recv.at[1, s], z_left))

    def ring_wait(s):
        from_left, from_right = (z + RING - s - 1) % RING, (z + s + 1) % RING
        if s < 3:
            a, b = shard(from_left), shard(from_right)
        else:
            a, b = shard(from_left, right_parts), shard(from_right, left_parts)
        wait_bytes(a, z_recv.at[0, s])
        wait_bytes(b, z_recv.at[1, s])

    ring_step(0)
    start_forward(0)
    residual = [
        pltpu.make_async_copy(source, target, local_sem.at[i])
        for i, (source, target) in enumerate(
            ((hidden, hid), (hidden_tan, hid_tan), (gate_table, gates), (gate_rate, rates))
        )
    ]
    for copy in residual:
        copy.start()
    start_forward(1)
    for s in range(1, 4):
        ring_wait(s - 1)
        ring_step(s)
    ring_wait(3)
    own_slab = slab(x, core)
    for k, peer in enumerate(x_peers):
        sends.append(remote(own_slab, own_slab, x_send.at[k], x_recv.at[k], peer))
    sends.append(remote(own_slab, own_slab, core_send.at[0], core_recv.at[0], sibling))

    def relay_slabs():
        for k in range(SIDE - 1):
            piece = slab((x + SIDE - 1 - k) % SIDE, core)
            wait_bytes(piece, x_recv.at[k])
            sends.append(remote(piece, piece, core_send.at[k + 1], core_recv.at[k + 1], sibling))

    def wait_slabs():
        for k in range(SIDE):
            wait_bytes(slab((x + SIDE - k) % SIDE, 1 - core), core_recv.at[k])

    for j in range(PARTS):
        wait_bytes(xbuf.at[j], fwd_recv.at[j])
        if j + AHEAD < PARTS:
            start_forward(j + AHEAD)
        attend(j)
        start_back(j)
        if j >= 1:
            start_tokens(j - 1)
        if j == 3:
            relay_slabs()
    wait_slabs()
    for j in range(3):
        wait_tokens(j)
        project(j)
    start_tokens(4)
    wait_tokens(3)
    project(3)
    wait_tokens(4)
    project(4)

    def send_tile(n):
        total = acc[n].astype(jnp.bfloat16).reshape(SIDE, 2, ROWS, TILE)
        out_send[n] = total
        for k, peer in enumerate(y_peers):
            remote(
                out_send.at[n, (y + k + 1) % SIDE],
                out_recv.at[n, y],
                res_send.at[n, k],
                res_recv.at[n, k],
                peer,
            )
        out_recv[n, y] = out_send[n, y]

    for n in range(TILES):
        send_tile(n)

    for copy in residual:
        copy.wait()
    level = timestep[0]
    levels = lax.broadcasted_iota(jnp.int32, gates.shape, 0)
    gate_row = jnp.sum(jnp.where(levels == level, gates[...], 0.0), axis=0, keepdims=True)
    rate_row = jnp.sum(jnp.where(levels == level, rates[...], 0.0), axis=0, keepdims=True)
    gates[0:1, :] = gate_row
    rates[0:1, :] = rate_row

    for n in range(TILES):
        for k in range(SIDE - 1):
            wait_bytes(out_recv.at[n, (y + SIDE - 1 - k) % SIDE], res_recv.at[n, k])
        for r in range(SIDE):
            columns = pl.ds(r * SLICE + n * TILE, TILE)
            gate, rate = gates[0:1, columns], rates[0:1, columns]
            value = out_recv[n, r, 0].astype(jnp.float32)
            value_tan = out_recv[n, r, 1].astype(jnp.float32)
            out[:, columns] = (hid[:, columns].astype(jnp.float32) + gate * value).astype(jnp.bfloat16)
            out_tan[:, columns] = (
                hid_tan[:, columns].astype(jnp.float32) + gate * value_tan + rate * value
            ).astype(jnp.bfloat16)

    for j in range(PARTS):
        wait_bytes(xbuf.at[j, :, pl.ds(0, LEN - ROWS), :], fwd_send.at[j])
        wait_bytes(att.at[j, :, pl.ds(0, LEN - ROWS), :], back_send.at[j])
        for k in range(SIDE - 1):
            wait_bytes(tok.at[j, y], tok_send.at[j, k])
    for copy in sends:
        copy.wait_send()
    for n in range(TILES):
        for k in range(SIDE - 1):
            wait_bytes(out_send.at[n, 0], res_send.at[n, k])


def shards(projected, projected_tan, hidden, hidden_tan, out_weight, gate_table, gate_rate, timestep):
    proj = jnp.transpose(projected, (0, 2, 1, 3)).reshape(3, ROWS, D)
    ptan = jnp.transpose(projected_tan, (0, 2, 1, 3)).reshape(3, ROWS, D)
    any_spec = pl.BlockSpec(memory_space=pl.ANY)
    vmem = pl.BlockSpec(memory_space=pltpu.VMEM)
    bf16 = jnp.bfloat16
    dma = pltpu.SemaphoreType.DMA
    block_out, block_tan = pl.pallas_call(
        kernel,
        out_shape=(jax.ShapeDtypeStruct((ROWS, D), bf16), jax.ShapeDtypeStruct((ROWS, D), bf16)),
        in_specs=[any_spec] * 7 + [pl.BlockSpec(memory_space=pltpu.SMEM)],
        out_specs=(vmem, vmem),
        scratch_shapes=[
            pltpu.VMEM((PARTS, 6, LEN, HEAD), bf16),
            pltpu.VMEM((PARTS, 2, LEN, HEAD), bf16),
            pltpu.VMEM((PARTS, SIDE, 2, ROWS, NT * HEAD), bf16),
            pltpu.VMEM((PARTS, SLICE, NT * HEAD), bf16),
            pltpu.VMEM((TILES, SIDE * 2 * ROWS, TILE), jnp.float32),
            pltpu.VMEM((TILES, SIDE, 2, ROWS, TILE), bf16),
            pltpu.VMEM((TILES, SIDE, 2, ROWS, TILE), bf16),
            pltpu.VMEM((ROWS, D), bf16),
            pltpu.VMEM((ROWS, D), bf16),
            pltpu.VMEM((32, D), jnp.float32),
            pltpu.VMEM((32, D), jnp.float32),
            dma((PARTS,)),
            dma((PARTS,)),
            dma((PARTS,)),
            dma((PARTS,)),
            dma((PARTS, SIDE - 1)),
            dma((PARTS, SIDE - 1)),
            dma((2, 4)),
            dma((2, 4)),
            dma((SIDE - 1,)),
            dma((SIDE - 1,)),
            dma((SIDE,)),
            dma((SIDE,)),
            dma((TILES, SIDE - 1)),
            dma((TILES, SIDE - 1)),
            dma((4,)),
            dma((1,)),
        ],
        compiler_params=pltpu.CompilerParams(
            collective_id=0, has_side_effects=True, vmem_limit_bytes=56 * 1024 * 1024
        ),
    )(
        proj,
        ptan,
        hidden.reshape(ROWS, D),
        hidden_tan.reshape(ROWS, D),
        out_weight.T,
        gate_table,
        gate_rate,
        timestep,
    )
    return block_out[None], block_tan[None]


def solution(mesh):
    return jax.shard_map(
        shards,
        mesh=mesh,
        in_specs=(
            P("dp", "tensor", None, None),
            P("dp", "tensor", None, None),
            P("dp", "tensor", None),
            P("dp", "tensor", None),
            P("tensor", "dp"),
            P(),
            P(),
            P("dp"),
        ),
        out_specs=(P("dp", "tensor", None), P("dp", "tensor", None)),
        check_vma=False,
    )
```

time: 364 us -> 197 us (0.54)
  waiting for transfers between devices: 230 us -> 0 us
  Pallas kernels: 0 us -> 191 us
  local copies, waits for them, and re-layouts: 73 us -> 3.93 us
  matrix products: 27.5 us -> 0 us
  between operations: 15 us -> 1.29 us
  starting transfers between devices: 12.1 us -> 0 us
    pallas_call x0 -> x1, Pallas kernels: none -> 191 us  [shards(): pl.pallas_call(kernel, out_shape=(jax.ShapeDtypeStruct((ROWS, D), bf16),...]
    all_to_all x2 -> x0, waiting for transfers between devices: 120 us -> none  [the longest x1 75.1 us: shards(): lax.all_to_all(projected_tan, 'tensor', split_axis=3, concat_axis=1, tile...]
    reduce_scatter x1 -> x0, waiting for transfers between devices: 109 us -> none  [shards(): lax.psum_scatter(partial_terms.astype(jnp.bfloat16), 'tensor', scatter_di...]
    unnamed x28 -> x2, local copies, waits for them, and re-layouts: 48.1 us -> 3.93 us
    dot_general x8 -> x0, matrix products: 21.6 us -> none  [the longest x1 14.1 us: shards(): jnp.einsum('bclh,hd->bcld', stacked, full_weight, preferred_element_type=...]
    all_to_all x2 -> x0, starting transfers between devices: 12.1 us -> none  [the longest x1 7.4 us: shards(): lax.all_to_all(projected, 'tensor', split_axis=3, concat_axis=1, tiled=True)]
    all_to_all x2 -> x0, local copies, waits for them, and re-layouts: 11.8 us -> none  [the longest x1 5.91 us: shards(): lax.all_to_all(projected, 'tensor', split_axis=3, concat_axis=1, tiled=True)]
    squeeze x2 -> x0, local copies, waits for them, and re-layouts: 7.01 us -> none  [shards(): attended, attended_tan = lax.map(attend_clip, (packed, packed_tan))]
  transfers between devices with their start and end apart: 4 -> 0, of which waited for: 3 -> 0; matrix products, arithmetic and copies ran while one was open for 23% -> 0% of each run, Pallas kernels for 0% -> 0%
where the time goes in v1:
time: 197 us; the launch traced here: 196 us
  Pallas kernels  191 us (97%)
  local copies, waits for them, and re-layouts  3.93 us (2%)
    pallas_call x1, Pallas kernels, shards(): pl.pallas_call(kernel, out_shape=(jax.ShapeDtypeStruct((ROWS, D), bf16),...  191 us

profile of v1, /device:TPU:1, one launch (start us, length us, event | category | flops | bytes accessed | tf_op | source)
XLA Modules:
  0.0 196.3 jit_solution(17766881355559706182)
XLA Ops:
  1.3 191.1 %shard_map.95 = (bf16[64,5120]{1,0:T(8,128)(2,1)}, bf16[64,5120]{1,0:T(8,128)(2,1)}) custom-call(bf16[3,64,5120]{2,1,0:T(8,128)(2,1)} %bitcast.11, bf16[3,64,5120]{2,1,0:T(8,128)(2,1)} %bitcast.12, bf16[64,5120]{1,0:T(8,128)(2,1)} %bitcast.15, bf16[64,5120]{1,0:T(8,128)(2,1)} %bitcast.16, bf16[160,640]{1,0:T(8,128)(2,1)} %bitcast.17, f32[32,5120]{1,0:T(8,128)} %gate_table.1, ...), custom_call_target="tpu_custom_call" | custom-call | tf_op jit(solution)/shard_map/pallas_call | solution.py:317
  192.4 2.0 %copy.13 = bf16[1,64,5120]{2,1,0:T(8,128)(2,1)} copy(bf16[1,64,5120]{2,1,0:T(8,128)(2,1)} %bitcast.14) | data formatting | bytes 1310720
  194.3 2.0 %copy.14 = bf16[1,64,5120]{2,1,0:T(8,128)(2,1)} copy(bf16[1,64,5120]{2,1,0:T(8,128)(2,1)} %bitcast.13) | data formatting | bytes 1310720

commit v2 on v1

v2 whole, which is shorter than its diff:
```python
import math

import jax
import jax.numpy as jnp
from jax import lax
from jax.experimental import pallas as pl
from jax.experimental.pallas import tpu as pltpu
from jax.sharding import PartitionSpec as P

HEAD = 128
PARTS = 5
LEN = 512
ROWS = 64
HALF = 32
NT = 8
SIDE = 4
RING = 8
COLS = 160
SLAB = 320
SLICE = 1280
TILES = 5
TILE = 256
D = 5120
BLOCK = 256
PEER_ORDER = (6, 4, 7, 5, 2, 3, 1)
SCALE = 1.0 / math.sqrt(HEAD)
MESH = pl.DeviceIdType.MESH
NT_DIMS = (((1,), (1,)), ((), ()))


def place(y, x, z, core):
    return (y * 8 + x * 2 + z // SIDE, (z % SIDE) * 2 + core)


def aligned(value, size, base):
    return pl.ds(pl.multiple_of(value, base), size)


def kernel(
    proj, ptan, hidden, hidden_tan, weight, gate_table, gate_rate, timestep,
    out, out_tan,
    xkv, xq, att, tok, wbuf, acc, out_send, out_recv, hid, hid_tan, gates, rates,
    kv_send, kv_recv, q_send, q_recv, back_send, back_recv, tok_send, tok_recv,
    z_send, z_recv, w_send, w_recv, res_send, res_recv, local_sem, own_sem,
):
    dp, me = lax.axis_index("dp"), lax.axis_index("tensor")
    y, x, z_hi = dp // 8, (dp % 8) // 2, dp % 2
    z_lo, core = me // 2, me % 2
    z = z_hi * SIDE + z_lo
    lanes = aligned((core * SIDE + z_lo) * HEAD, HEAD, HEAD)

    def pick(which_core, first, second):
        return first * (1 - which_core) + second * which_core

    rank, own_slot = pick(core, y, x), pick(core, x, y)
    z_right = place(y, x, (z + 1) % RING, core)
    z_left = place(y, x, (z + RING - 1) % RING, core)

    def along_x(k, which_core):
        return place(y, (x + k) % SIDE, z, which_core)

    def along_y(k, which_core):
        return place((y + k) % SIDE, x, z, which_core)

    def row_peer(k):
        return place(pick(core, (y + k) % SIDE, y), pick(core, x, (x + k) % SIDE), z, core)

    def weight_peer(k, which_core):
        return place(pick(which_core, y, (y + k) % SIDE), pick(which_core, (x + k) % SIDE, x), z, which_core)

    def remote(src, dst, send, recv, device):
        copy = pltpu.make_async_remote_copy(
            src_ref=src, dst_ref=dst, send_sem=send, recv_sem=recv, device_id=device, device_id_type=MESH
        )
        copy.start()
        return copy

    def wait_bytes(ref, sem):
        pltpu.make_async_copy(ref, ref, sem).wait()

    barrier = pltpu.get_barrier_semaphore()
    greeted = [(dp, (me + k) % NT) for k in range(1, NT)] + [z_right, z_left]
    for k in range(1, SIDE):
        greeted += [along_x(k, 0), along_x(k, 1), along_y(k, 0), along_y(k, 1)]
    for device in greeted:
        pl.semaphore_signal(barrier, inc=1, device_id=device, device_id_type=MESH)
    own_copies = [
        pltpu.make_async_copy(
            weight.at[:, pl.ds(j * HEAD, HEAD)],
            wbuf.at[j, aligned(own_slot * SLAB + z_hi * COLS, COLS, COLS), lanes],
            own_sem.at[0],
        )
        for j in range(PARTS)
    ]
    for copy in own_copies:
        copy.start()
    residual = [
        pltpu.make_async_copy(source, target, local_sem.at[i])
        for i, (source, target) in enumerate(
            ((hidden, hid), (hidden_tan, hid_tan), (gate_table, gates), (gate_rate, rates))
        )
    ]
    for copy in residual:
        copy.start()
    pl.semaphore_wait(barrier, len(greeted))

    def xor_peer(k):
        result = 0
        for bit in (1, 2, 4):
            mine = (me // bit) % 2
            result = result + bit * ((1 - mine) if k & bit else mine)
        return result

    peers = [xor_peer(k) for k in PEER_ORDER]

    def head_columns(peer, j):
        return aligned((peer * PARTS + j) * HEAD, HEAD, HEAD)

    def start_kv(j):
        for peer in peers:
            for half, source in enumerate((proj, ptan)):
                remote(
                    source.at[pl.ds(1, 2), :, :, head_columns(peer, j)],
                    xkv.at[j, pl.ds(2 * half, 2), me],
                    kv_send.at[j],
                    kv_recv.at[j],
                    (dp, peer),
                )
        for half, source in enumerate((proj, ptan)):
            pltpu.make_async_copy(
                source.at[pl.ds(1, 2), :, :, head_columns(me, j)], xkv.at[j, pl.ds(2 * half, 2), me], kv_recv.at[j]
            ).start()

    def q_index(j, b):
        return j if b is None else j + b

    def start_q(j, b=None):
        blocks = pl.ds(0, 2) if b is None else pl.ds(b, 1)
        i = q_index(j, b)
        for peer in peers:
            for half, source in enumerate((proj, ptan)):
                remote(
                    source.at[0, blocks, :, head_columns(peer, j)],
                    xq.at[j, half, blocks, me],
                    q_send.at[i],
                    q_recv.at[i],
                    (dp, peer),
                )
        for half, source in enumerate((proj, ptan)):
            pltpu.make_async_copy(
                source.at[0, blocks, :, head_columns(me, j)], xq.at[j, half, blocks, me], q_recv.at[i]
            ).start()

    def wait_kv(j):
        wait_bytes(xkv.at[j], kv_recv.at[j])

    def wait_q(j, b=None):
        blocks = pl.ds(0, 2) if b is None else pl.ds(b, 1)
        wait_bytes(xq.at[j, :, blocks], q_recv.at[q_index(j, b)])

    def start_back(j, b=None):
        blocks = pl.ds(0, 2) if b is None else pl.ds(b, 1)
        i = q_index(j, b)
        for peer in peers:
            remote(
                att.at[j, blocks, :, peer],
                tok.at[j, pick(peer % 2, y, x), blocks, :, :, lanes],
                back_send.at[i],
                back_recv.at[i],
                (dp, peer),
            )
        pltpu.make_async_copy(att.at[j, blocks, :, me], tok.at[j, rank, blocks, :, :, lanes], back_recv.at[i]).start()

    def start_tokens(j, b=None):
        blocks = pl.ds(0, 2) if b is None else pl.ds(b, 1)
        i = q_index(j, b)
        mine = tok.at[j, rank, blocks]
        wait_bytes(mine, back_recv.at[i])
        for k in range(1, SIDE):
            remote(mine, mine, tok_send.at[i, k - 1], tok_recv.at[i, k - 1], row_peer(k))

    def wait_tokens(j, b=None):
        blocks = pl.ds(0, 2) if b is None else pl.ds(b, 1)
        for k in range(1, SIDE):
            wait_bytes(tok.at[j, (rank + SIDE - k) % SIDE, blocks], tok_recv.at[q_index(j, b), k - 1])

    def attend(j, b):
        q = xq[j, 0, b].reshape(BLOCK, HEAD)
        qt = xq[j, 1, b].reshape(BLOCK, HEAD)
        k, v, kt, vt = (xkv[j, i].reshape(LEN, HEAD) for i in range(4))
        s = lax.dot_general(q, k, NT_DIMS, preferred_element_type=jnp.float32)
        st = lax.dot_general(
            jnp.concatenate([qt, q], axis=1),
            jnp.concatenate([k, kt], axis=1),
            NT_DIMS,
            preferred_element_type=jnp.float32,
        )
        top = jnp.max(s, axis=-1, keepdims=True)
        e = jnp.exp2((s - top) * (SCALE * math.log2(math.e)))
        probs = e * (1.0 / jnp.sum(e, axis=-1, keepdims=True))
        low = probs.astype(jnp.bfloat16)
        mean = jnp.sum(probs * st, axis=-1, keepdims=True)
        probs_tan = (probs * ((st - mean) * SCALE)).astype(jnp.bfloat16)
        both = jnp.dot(low, jnp.concatenate([v, vt], axis=1), preferred_element_type=jnp.float32)
        tan = jnp.dot(probs_tan, v, preferred_element_type=jnp.float32) + both[:, HEAD:]
        att[j, b, 0] = both[:, :HEAD].astype(jnp.bfloat16).reshape(NT, HALF, HEAD)
        att[j, b, 1] = tan.astype(jnp.bfloat16).reshape(NT, HALF, HEAD)

    def attend_all(j):
        def block(b, carry):
            attend(j, b)
            return carry

        lax.fori_loop(0, 2, block, 0)

    def project(j):
        rows = tok[j].reshape(SIDE * 2 * 2 * HALF, NT * HEAD)

        def tile(n, carry):
            part = lax.dot_general(
                rows,
                wbuf[j, aligned(n * TILE, TILE, TILE), :],
                NT_DIMS,
                preferred_element_type=jnp.float32,
            ).reshape(SIDE, 2, 2 * HALF, TILE)
            if j == 0:
                acc[n] = part
            else:
                acc[n] = acc[n] + part
            return carry

        lax.fori_loop(0, TILES, tile, 0)

    def project_last(j, b):
        rows = tok[j, :, b].reshape(SIDE * 2 * HALF, NT * HEAD)

        def tile(n, carry):
            part = lax.dot_general(
                rows,
                wbuf[j, aligned(n * TILE, TILE, TILE), :],
                NT_DIMS,
                preferred_element_type=jnp.float32,
            ).reshape(SIDE, 2 * HALF, TILE)
            total = (acc[n, :, b] + part).astype(jnp.bfloat16).reshape(SIDE, 2, HALF, TILE)
            out_send[b, :, n] = total
            return carry

        lax.fori_loop(0, TILES, tile, 0)
        for k in range(1, SIDE):
            remote(
                out_send.at[b, (rank + k) % SIDE],
                out_recv.at[b, rank],
                res_send.at[b, k - 1],
                res_recv.at[b, k - 1],
                row_peer(k),
            )
        out_recv[b, rank] = out_send[b, rank]

    def shard(slot, which, parts=pl.ds(0, PARTS)):
        return wbuf.at[
            parts,
            aligned(slot * SLAB + (which // SIDE) * COLS, COLS, COLS),
            aligned((core * SIDE + which % SIDE) * HEAD, HEAD, HEAD),
        ]

    def slab(slot, which_core):
        return wbuf.at[
            :, aligned(slot * SLAB, SLAB, SLAB), aligned(which_core * SIDE * HEAD, SIDE * HEAD, SIDE * HEAD)
        ]

    right_parts, left_parts = pl.ds(0, 3), pl.ds(3, 2)
    ring_sends = []

    def ring_step(s):
        a, b = (z + RING - s) % RING, (z + s) % RING
        if s < 3:
            a, b = shard(own_slot, a), shard(own_slot, b)
        else:
            a, b = shard(own_slot, a, right_parts), shard(own_slot, b, left_parts)
        ring_sends.append(remote(a, a, z_send.at[0, s], z_recv.at[0, s], z_right))
        ring_sends.append(remote(b, b, z_send.at[1, s], z_recv.at[1, s], z_left))

    def fan(which):
        source = shard(own_slot, which)
        for k in range(1, SIDE):
            remote(source, source, w_send.at[k - 1], w_recv.at[k - 1], weight_peer(k, core))
        other = shard(pick(core, y, x), which)
        for k in range(SIDE):
            remote(source, other, w_send.at[3 + k], w_recv.at[3 + k], weight_peer(k, 1 - core))

    def ring_wait(s):
        from_left, from_right = (z + RING - s - 1) % RING, (z + s + 1) % RING
        if s < 3:
            a, b = shard(own_slot, from_left), shard(own_slot, from_right)
        else:
            a, b = shard(own_slot, from_left, right_parts), shard(own_slot, from_right, left_parts)
        wait_bytes(a, z_recv.at[0, s])
        wait_bytes(b, z_recv.at[1, s])
        if s < 3:
            ring_step(s + 1)
            fan(from_left)
            fan(from_right)
        else:
            fan(from_left)

    def wait_weights():
        for k in range(1, SIDE):
            wait_bytes(slab((own_slot + SIDE - k) % SIDE, core), w_recv.at[k - 1])
        for k in range(SIDE):
            wait_bytes(slab((own_slot + SIDE - k) % SIDE, 1 - core), w_recv.at[3 + k])

    wait_bytes(shard(own_slot, z), own_sem.at[0])
    ring_step(0)
    start_kv(0)
    start_q(0)
    fan(z)
    ring_wait(0)
    wait_kv(0)
    start_kv(1)
    ring_wait(1)
    wait_q(0)
    start_q(1)
    attend_all(0)
    start_back(0)
    ring_wait(2)
    wait_kv(1)
    start_kv(2)
    ring_wait(3)
    wait_q(1)
    start_q(2)
    attend_all(1)
    start_back(1)
    start_tokens(0)
    wait_kv(2)
    start_kv(3)
    wait_q(2)
    start_q(3)
    attend_all(2)
    start_back(2)
    start_tokens(1)
    wait_kv(3)
    start_kv(4)
    wait_q(3)
    start_q(4, 0)
    start_q(4, 1)
    attend_all(3)
    start_back(3)
    start_tokens(2)
    wait_weights()
    for j in range(2):
        wait_tokens(j)
        project(j)
    wait_kv(4)
    wait_q(4, 0)
    attend(4, 0)
    start_back(4, 0)
    start_tokens(3)
    wait_q(4, 1)
    attend(4, 1)
    start_back(4, 1)
    wait_tokens(2)
    project(2)
    start_tokens(4, 0)
    wait_tokens(3)
    project(3)
    start_tokens(4, 1)
    wait_tokens(4, 0)
    project_last(4, 0)
    wait_tokens(4, 1)
    project_last(4, 1)

    for copy in residual:
        copy.wait()
    level = timestep[0]
    levels = lax.broadcasted_iota(jnp.int32, gates.shape, 0)
    gate_row = jnp.sum(jnp.where(levels == level, gates[...], 0.0), axis=0, keepdims=True)
    rate_row = jnp.sum(jnp.where(levels == level, rates[...], 0.0), axis=0, keepdims=True)
    gates[0:1, :] = gate_row
    rates[0:1, :] = rate_row

    def finish(b, columns, value, value_tan):
        rows = pl.ds(b * HALF, HALF)
        gate, rate = gates[0:1, columns], rates[0:1, columns]
        out[rows, columns] = (hid[rows, columns].astype(jnp.float32) + gate * value).astype(jnp.bfloat16)
        out_tan[rows, columns] = (
            hid_tan[rows, columns].astype(jnp.float32) + gate * value_tan + rate * value
        ).astype(jnp.bfloat16)

    def finish_straight(b):
        for r in range(SIDE):
            for n in range(TILES):
                value = out_recv[b, r, n].astype(jnp.float32)
                finish(b, pl.ds(r * SLICE + n * TILE, TILE), value[0], value[1])

    def finish_crossed(b):
        lower = lax.broadcasted_iota(jnp.int32, (2 * HALF, HEAD), 1) < HEAD // 2

        def load(r, unit):
            q = unit // 2
            piece = out_recv[b, r, q // 2, :, :, pl.ds((q % 2) * HEAD, HEAD)]
            return piece.astype(jnp.float32).reshape(2 * HALF, HEAD)

        for t in range(D // HEAD):
            found = []
            for g in (2 * t, 2 * t + 1):
                s, rest = g // 20, g % 20
                found.append((rest // 5, 5 * s + rest % 5))
            (r0, u0), (r1, u1) = found
            first = load(r0, u0)
            if u0 % 2:
                first = pltpu.roll(first, HEAD // 2, 1)
            if r0 == r1 and u0 % 2 == 0 and u1 == u0 + 1:
                value = first
            else:
                second = load(r1, u1)
                if u1 % 2 == 0:
                    second = pltpu.roll(second, HEAD // 2, 1)
                value = jnp.where(lower, first, second)
            finish(b, pl.ds(t * HEAD, HEAD), value[:HALF], value[HALF:])

    for b in range(2):
        for k in range(1, SIDE):
            wait_bytes(out_recv.at[b, (rank + SIDE - k) % SIDE], res_recv.at[b, k - 1])
        pl.when(core == 0)(lambda b=b: finish_straight(b))
        pl.when(core == 1)(lambda b=b: finish_crossed(b))

    for j in range(PARTS):
        wait_bytes(xkv.at[j, :, pl.ds(0, NT - 1)], kv_send.at[j])
        for b in (None,) if j < PARTS - 1 else (0, 1):
            blocks = pl.ds(0, 2) if b is None else pl.ds(b, 1)
            i = q_index(j, b)
            wait_bytes(xq.at[j, :, blocks, pl.ds(0, NT - 1)], q_send.at[i])
            wait_bytes(att.at[j, blocks, :, pl.ds(0, NT - 1)], back_send.at[i])
            for k in range(SIDE - 1):
                wait_bytes(tok.at[j, rank, blocks], tok_send.at[i, k])
    for copy in ring_sends:
        copy.wait_send()
    for k in range(7):
        wait_bytes(slab(own_slot, core), w_send.at[k])
    for b in range(2):
        for k in range(SIDE - 1):
            wait_bytes(out_send.at[b, 0], res_send.at[b, k])


def shards(projected, projected_tan, hidden, hidden_tan, out_weight, gate_table, gate_rate, timestep):
    proj = jnp.transpose(projected, (0, 2, 1, 3)).reshape(3, 2, HALF, D)
    ptan = jnp.transpose(projected_tan, (0, 2, 1, 3)).reshape(3, 2, HALF, D)
    any_spec = pl.BlockSpec(memory_space=pl.ANY)
    vmem = pl.BlockSpec(memory_space=pltpu.VMEM)
    bf16 = jnp.bfloat16
    dma = pltpu.SemaphoreType.DMA
    block_out, block_tan = pl.pallas_call(
        kernel,
        out_shape=(jax.ShapeDtypeStruct((ROWS, D), bf16), jax.ShapeDtypeStruct((ROWS, D), bf16)),
        in_specs=[any_spec] * 7 + [pl.BlockSpec(memory_space=pltpu.SMEM)],
        out_specs=(vmem, vmem),
        scratch_shapes=[
            pltpu.VMEM((PARTS, 4, NT, 2, HALF, HEAD), bf16),
            pltpu.VMEM((PARTS, 2, 2, NT, HALF, HEAD), bf16),
            pltpu.VMEM((PARTS, 2, 2, NT, HALF, HEAD), bf16),
            pltpu.VMEM((PARTS, SIDE, 2, 2, HALF, NT * HEAD), bf16),
            pltpu.VMEM((PARTS, SLICE, NT * HEAD), bf16),
            pltpu.VMEM((TILES, SIDE, 2, 2 * HALF, TILE), jnp.float32),
            pltpu.VMEM((2, SIDE, TILES, 2, HALF, TILE), bf16),
            pltpu.VMEM((2, SIDE, TILES, 2, HALF, TILE), bf16),
            pltpu.VMEM((ROWS, D), bf16),
            pltpu.VMEM((ROWS, D), bf16),
            pltpu.VMEM((32, D), jnp.float32),
            pltpu.VMEM((32, D), jnp.float32),
            dma((PARTS,)),
            dma((PARTS,)),
            dma((PARTS + 1,)),
            dma((PARTS + 1,)),
            dma((PARTS + 1,)),
            dma((PARTS + 1,)),
            dma((PARTS + 1, SIDE - 1)),
            dma((PARTS + 1, SIDE - 1)),
            dma((2, 4)),
            dma((2, 4)),
            dma((7,)),
            dma((7,)),
            dma((2, SIDE - 1)),
            dma((2, SIDE - 1)),
            dma((4,)),
            dma((1,)),
        ],
        compiler_params=pltpu.CompilerParams(
            collective_id=0, has_side_effects=True, vmem_limit_bytes=56 * 1024 * 1024
        ),
    )(
        proj,
        ptan,
        hidden.reshape(ROWS, D),
        hidden_tan.reshape(ROWS, D),
        out_weight.T,
        gate_table,
        gate_rate,
        timestep,
    )
    return block_out[None], block_tan[None]


def solution(mesh):
    return jax.shard_map(
        shards,
        mesh=mesh,
        in_specs=(
            P("dp", "tensor", None, None),
            P("dp", "tensor", None, None),
            P("dp", "tensor", None),
            P("dp", "tensor", None),
            P("tensor", "dp"),
            P(),
            P(),
            P("dp"),
        ),
        out_specs=(P("dp", "tensor", None), P("dp", "tensor", None)),
        check_vma=False,
    )
```

time: 197 us -> 166 us (0.84)
  Pallas kernels: 191 us -> 160 us
    pallas_call x1, Pallas kernels: 191 us -> 160 us  [shards(): pl.pallas_call(kernel, out_shape=(jax.ShapeDtypeStruct((ROWS, D), bf16),...]
where the time goes in v2:
time: 166 us; the launch traced here: 165 us
  Pallas kernels  160 us (96%)
  local copies, waits for them, and re-layouts  3.93 us (2%)
    pallas_call x1, Pallas kernels, shards(): pl.pallas_call(kernel, out_shape=(jax.ShapeDtypeStruct((ROWS, D), bf16),...  160 us
    unnamed x2, local copies, waits for them, and re-layouts  3.93 us

profile of v2, /device:TPU:1, one launch (start us, length us, event | category | flops | bytes accessed | tf_op | source)
XLA Modules:
  0.0 165.4 jit_solution(8873388467273506362)
XLA Ops:
  1.3 160.1 %shard_map.95 = (bf16[64,5120]{1,0:T(8,128)(2,1)}, bf16[64,5120]{1,0:T(8,128)(2,1)}) custom-call(bf16[3,2,32,5120]{3,2,1,0:T(8,128)(2,1)} %bitcast.11, bf16[3,2,32,5120]{3,2,1,0:T(8,128)(2,1)} %bitcast.12, bf16[64,5120]{1,0:T(8,128)(2,1)} %bitcast.15, bf16[64,5120]{1,0:T(8,128)(2,1)} %bitcast.16, bf16[160,640]{1,0:T(8,128)(2,1)} %bitcast.17, ...), custom_call_target="tpu_custom_call" | custom-call | tf_op jit(solution)/shard_map/pallas_call | solution.py:452
  161.4 2.0 %copy.13 = bf16[1,64,5120]{2,1,0:T(8,128)(2,1)} copy(bf16[1,64,5120]{2,1,0:T(8,128)(2,1)} %bitcast.14) | data formatting | bytes 1310720
  163.4 2.0 %copy.14 = bf16[1,64,5120]{2,1,0:T(8,128)(2,1)} copy(bf16[1,64,5120]{2,1,0:T(8,128)(2,1)} %bitcast.13) | data formatting | bytes 1310720

commit v3 on v2

v3 whole, which is shorter than its diff:
```python
import math

import jax
import jax.numpy as jnp
from jax import lax
from jax.experimental import pallas as pl
from jax.experimental.pallas import tpu as pltpu
from jax.sharding import PartitionSpec as P

HEAD = 128
PARTS = 5
LEN = 512
ROWS = 64
BLOCKS = 4
UNIT = ROWS // BLOCKS
ALL = (0, BLOCKS)
GROUPS = ((0, 2), (2, 2))
LAST = 4
NT = 8
SIDE = 4
RING = 8
COLS = 160
SLAB = 320
SLICE = 1280
TILES = 5
TILE = 256
D = 5120
PEER_ORDER = (2, 3, 4, 5, 6, 7, 1)
SCALE = 1.0 / math.sqrt(HEAD)
MESH = pl.DeviceIdType.MESH
NT_DIMS = (((1,), (1,)), ((), ()))


def place(y, x, z, core):
    return (y * 8 + x * 2 + z // SIDE, (z % SIDE) * 2 + core)


def aligned(value, size, base):
    return pl.ds(pl.multiple_of(value, base), size)


def kernel(
    proj, ptan, hidden, hidden_tan, weight, gate_table, gate_rate, timestep,
    out, out_tan,
    xkv, xq, att, tok, wbuf, acc, out_send, out_recv, hid, hid_tan, gates, rates,
    kv_send, kv_recv, q_send, q_recv, back_send, back_recv, tok_send, tok_recv,
    z_send, z_recv, w_send, w_recv, res_send, res_recv, local_sem, own_sem,
):
    dp, me = lax.axis_index("dp"), lax.axis_index("tensor")
    y, x, z_hi = dp // 8, (dp % 8) // 2, dp % 2
    z_lo, core = me // 2, me % 2
    z = z_hi * SIDE + z_lo
    lanes = aligned((core * SIDE + z_lo) * HEAD, HEAD, HEAD)

    def pick(which_core, first, second):
        return first * (1 - which_core) + second * which_core

    rank, own_slot = pick(core, y, x), pick(core, x, y)
    z_right = place(y, x, (z + 1) % RING, core)
    z_left = place(y, x, (z + RING - 1) % RING, core)

    def along_x(k, which_core):
        return place(y, (x + k) % SIDE, z, which_core)

    def along_y(k, which_core):
        return place((y + k) % SIDE, x, z, which_core)

    def row_peer(k):
        return place(pick(core, (y + k) % SIDE, y), pick(core, x, (x + k) % SIDE), z, core)

    def weight_peer(k, which_core):
        return place(pick(which_core, y, (y + k) % SIDE), pick(which_core, (x + k) % SIDE, x), z, which_core)

    def remote(src, dst, send, recv, device):
        copy = pltpu.make_async_remote_copy(
            src_ref=src, dst_ref=dst, send_sem=send, recv_sem=recv, device_id=device, device_id_type=MESH
        )
        copy.start()
        return copy

    def wait_bytes(ref, sem):
        pltpu.make_async_copy(ref, ref, sem).wait()

    barrier = pltpu.get_barrier_semaphore()
    greeted = [(dp, (me + k) % NT) for k in range(1, NT)] + [z_right, z_left]
    for k in range(1, SIDE):
        greeted += [along_x(k, 0), along_x(k, 1), along_y(k, 0), along_y(k, 1)]
    for device in greeted:
        pl.semaphore_signal(barrier, inc=1, device_id=device, device_id_type=MESH)
    own_copies = [
        pltpu.make_async_copy(
            weight.at[:, pl.ds(j * HEAD, HEAD)],
            wbuf.at[j, aligned(own_slot * SLAB + z_hi * COLS, COLS, COLS), lanes],
            own_sem.at[0],
        )
        for j in range(PARTS)
    ]
    for copy in own_copies:
        copy.start()
    residual = [
        pltpu.make_async_copy(source, target, local_sem.at[i])
        for i, (source, target) in enumerate(
            ((hidden, hid), (hidden_tan, hid_tan), (gate_table, gates), (gate_rate, rates))
        )
    ]
    for copy in residual:
        copy.start()
    pl.semaphore_wait(barrier, len(greeted))

    def xor_peer(k):
        result = 0
        for bit in (1, 2, 4):
            mine = (me // bit) % 2
            result = result + bit * ((1 - mine) if k & bit else mine)
        return result

    peers = [xor_peer(k) for k in PEER_ORDER]

    def head_columns(peer, j):
        return aligned((peer * PARTS + j) * HEAD, HEAD, HEAD)

    def start_kv(j, half):
        source = (proj, ptan)[half]
        target = xkv.at[j, pl.ds(2 * half, 2), me]
        for peer in peers:
            remote(
                source.at[pl.ds(1, 2), :, :, head_columns(peer, j)],
                target,
                kv_send.at[j, half],
                kv_recv.at[j, half],
                (dp, peer),
            )
        pltpu.make_async_copy(
            source.at[pl.ds(1, 2), :, :, head_columns(me, j)], target, kv_recv.at[j, half]
        ).start()

    def wait_kv(j, half):
        wait_bytes(xkv.at[j, pl.ds(2 * half, 2)], kv_recv.at[j, half])

    def slot(j, group):
        return j if group is None else LAST + group

    def span(group):
        return pl.ds(*(ALL if group is None else GROUPS[group]))

    def start_q(j, group=None):
        blocks, i = span(group), slot(j, group)
        for peer in peers:
            for half, source in enumerate((proj, ptan)):
                remote(
                    source.at[0, blocks, :, head_columns(peer, j)],
                    xq.at[j, half, blocks, me],
                    q_send.at[i],
                    q_recv.at[i],
                    (dp, peer),
                )
        for half, source in enumerate((proj, ptan)):
            pltpu.make_async_copy(
                source.at[0, blocks, :, head_columns(me, j)], xq.at[j, half, blocks, me], q_recv.at[i]
            ).start()

    def wait_q(j, group=None):
        wait_bytes(xq.at[j, :, span(group)], q_recv.at[slot(j, group)])

    def start_back(j, group=None):
        blocks, i = span(group), slot(j, group)
        for peer in peers:
            remote(
                att.at[j, blocks, :, peer],
                tok.at[j, pick(peer % 2, y, x), blocks, :, :, lanes],
                back_send.at[i],
                back_recv.at[i],
                (dp, peer),
            )
        pltpu.make_async_copy(att.at[j, blocks, :, me], tok.at[j, rank, blocks, :, :, lanes], back_recv.at[i]).start()

    def start_tokens(j, group=None):
        i = slot(j, group)
        mine = tok.at[j, rank, span(group)]
        wait_bytes(mine, back_recv.at[i])
        for k in range(1, SIDE):
            remote(mine, mine, tok_send.at[i, k - 1], tok_recv.at[i, k - 1], row_peer(k))

    def wait_tokens(j, group=None):
        for k in range(1, SIDE):
            wait_bytes(tok.at[j, (rank + SIDE - k) % SIDE, span(group)], tok_recv.at[slot(j, group), k - 1])

    def attend(j, first, count):
        blocks, rows = pl.ds(first, count), count * NT * UNIT
        q = xq[j, 0, blocks].reshape(rows, HEAD)
        qt = xq[j, 1, blocks].reshape(rows, HEAD)
        k, v, kt, vt = (xkv[j, i].reshape(LEN, HEAD) for i in range(4))
        s = lax.dot_general(q, k, NT_DIMS, preferred_element_type=jnp.float32)
        st = lax.dot_general(
            jnp.concatenate([qt, q], axis=1),
            jnp.concatenate([k, kt], axis=1),
            NT_DIMS,
            preferred_element_type=jnp.float32,
        )
        top = jnp.max(s, axis=-1, keepdims=True)
        e = jnp.exp2((s - top) * (SCALE * math.log2(math.e)))
        probs = e * (1.0 / jnp.sum(e, axis=-1, keepdims=True))
        low = probs.astype(jnp.bfloat16)
        mean = jnp.sum(probs * st, axis=-1, keepdims=True)
        probs_tan = (probs * ((st - mean) * SCALE)).astype(jnp.bfloat16)
        both = jnp.dot(low, jnp.concatenate([v, vt], axis=1), preferred_element_type=jnp.float32)
        tan = jnp.dot(probs_tan, v, preferred_element_type=jnp.float32) + both[:, HEAD:]
        att[j, blocks, 0] = both[:, :HEAD].astype(jnp.bfloat16).reshape(count, NT, UNIT, HEAD)
        att[j, blocks, 1] = tan.astype(jnp.bfloat16).reshape(count, NT, UNIT, HEAD)

    def attend_all(j):
        attend(j, *ALL)

    def project(j):
        rows = tok[j].reshape(SIDE * 2 * ROWS, NT * HEAD)

        def tile(n, carry):
            part = lax.dot_general(
                rows,
                wbuf[j, aligned(n * TILE, TILE, TILE), :],
                NT_DIMS,
                preferred_element_type=jnp.float32,
            ).reshape(SIDE, BLOCKS, 2 * UNIT, TILE)
            if j == 0:
                acc[n] = part
            else:
                acc[n] = acc[n] + part
            return carry

        lax.fori_loop(0, TILES, tile, 0)

    def project_last(group):
        first, count = GROUPS[group]
        rows = tok[LAST, :, first : first + count].reshape(SIDE * count * 2 * UNIT, NT * HEAD)

        def tile(n, carry):
            part = lax.dot_general(
                rows,
                wbuf[LAST, aligned(n * TILE, TILE, TILE), :],
                NT_DIMS,
                preferred_element_type=jnp.float32,
            ).reshape(SIDE, count, 2 * UNIT, TILE)
            for b in range(count):
                total = (acc[n, :, first + b] + part[:, b]).astype(jnp.bfloat16)
                out_send[first + b, :, n] = total.reshape(SIDE, 2, UNIT, TILE)
            return carry

        lax.fori_loop(0, TILES, tile, 0)
        blocks = pl.ds(first, count)
        for k in range(1, SIDE):
            remote(
                out_send.at[blocks, (rank + k) % SIDE],
                out_recv.at[blocks, rank],
                res_send.at[group, k - 1],
                res_recv.at[group, k - 1],
                row_peer(k),
            )
        out_recv[blocks, rank] = out_send[blocks, rank]

    def shard(slot, which, parts=pl.ds(0, PARTS)):
        return wbuf.at[
            parts,
            aligned(slot * SLAB + (which // SIDE) * COLS, COLS, COLS),
            aligned((core * SIDE + which % SIDE) * HEAD, HEAD, HEAD),
        ]

    def slab(slot, which_core):
        return wbuf.at[
            :, aligned(slot * SLAB, SLAB, SLAB), aligned(which_core * SIDE * HEAD, SIDE * HEAD, SIDE * HEAD)
        ]

    def reach(which, direction):
        return (5 - which % SIDE) if direction == 0 else (2 + which % SIDE)

    def ring_copy(which, direction, s):
        piece = shard(own_slot, which)
        return pltpu.make_async_remote_copy(
            src_ref=piece,
            dst_ref=piece,
            send_sem=z_send.at[direction, s],
            recv_sem=z_recv.at[direction, s],
            device_id=(z_right, z_left)[direction],
            device_id_type=MESH,
        )

    def fan(which):
        source = shard(own_slot, which)
        for k in range(1, SIDE):
            remote(source, source, w_send.at[k - 1], w_recv.at[k - 1], weight_peer(k, core))
        other = shard(pick(core, y, x), which)
        for k in range(SIDE):
            remote(source, other, w_send.at[3 + k], w_recv.at[3 + k], weight_peer(k, 1 - core))

    def ring_wait(s):
        for direction in range(2):
            which = ((z + RING - s - 1) if direction == 0 else (z + s + 1)) % RING

            def arrived(which=which, direction=direction):
                wait_bytes(shard(own_slot, which), z_recv.at[direction, s])
                if s == 0:
                    ring_copy(which, direction, 1).start()
                elif s < 4:
                    pl.when(s + 1 < reach(which, direction))(lambda: ring_copy(which, direction, s + 1).start())
                fan(which)

            if s < 2:
                arrived()
            else:
                pl.when(s < reach(which, direction))(arrived)

    def wait_weights():
        for k in range(1, SIDE):
            wait_bytes(slab((own_slot + SIDE - k) % SIDE, core), w_recv.at[k - 1])
        for k in range(SIDE):
            wait_bytes(slab((own_slot + SIDE - k) % SIDE, 1 - core), w_recv.at[3 + k])

    wait_bytes(shard(own_slot, z), own_sem.at[0])
    for direction in range(2):
        ring_copy(z, direction, 0).start()
    start_kv(0, 0)
    start_kv(0, 1)
    start_q(0)
    fan(z)
    last = len(GROUPS)
    for j in range(PARTS - 1):
        for half in range(2):
            if 2 * j + half < 5:
                ring_wait(2 * j + half)
            wait_kv(j, half)
            start_kv(j + 1, half)
        wait_q(j)
        attend_all(j)
        start_back(j)
        if j + 1 < LAST:
            start_q(j + 1)
        if j >= 1:
            start_tokens(j - 1)
    wait_weights()
    for j in range(2):
        wait_tokens(j)
        project(j)
    wait_kv(LAST, 0)
    start_q(LAST, 0)
    wait_kv(LAST, 1)
    for group in range(1, last):
        start_q(LAST, group)
    start_tokens(3)
    wait_tokens(2)
    project(2)
    for group in range(last):
        wait_q(LAST, group)
        attend(LAST, *GROUPS[group])
        start_back(LAST, group)
        if group >= 1:
            start_tokens(LAST, group - 1)
    start_tokens(LAST, last - 1)
    wait_tokens(3)
    project(3)
    for group in range(last):
        wait_tokens(LAST, group)
        project_last(group)

    for copy in residual:
        copy.wait()
    level = timestep[0]
    levels = lax.broadcasted_iota(jnp.int32, gates.shape, 0)
    gate_row = jnp.sum(jnp.where(levels == level, gates[...], 0.0), axis=0, keepdims=True)
    rate_row = jnp.sum(jnp.where(levels == level, rates[...], 0.0), axis=0, keepdims=True)
    gates[0:1, :] = gate_row
    rates[0:1, :] = rate_row

    def finish(b, columns, value, value_tan):
        rows = pl.ds(b * UNIT, UNIT)
        gate, rate = gates[0:1, columns], rates[0:1, columns]
        out[rows, columns] = (hid[rows, columns].astype(jnp.float32) + gate * value).astype(jnp.bfloat16)
        out_tan[rows, columns] = (
            hid_tan[rows, columns].astype(jnp.float32) + gate * value_tan + rate * value
        ).astype(jnp.bfloat16)

    def finish_straight(b):
        for r in range(SIDE):
            for n in range(TILES):
                value = out_recv[b, r, n].astype(jnp.float32)
                finish(b, pl.ds(r * SLICE + n * TILE, TILE), value[0], value[1])

    def finish_crossed(b):
        lower = lax.broadcasted_iota(jnp.int32, (2 * UNIT, HEAD), 1) < HEAD // 2

        def load(r, unit):
            q = unit // 2
            piece = out_recv[b, r, q // 2, :, :, pl.ds((q % 2) * HEAD, HEAD)]
            return piece.astype(jnp.float32).reshape(2 * UNIT, HEAD)

        for t in range(D // HEAD):
            found = []
            for g in (2 * t, 2 * t + 1):
                s, rest = g // 20, g % 20
                found.append((rest // 5, 5 * s + rest % 5))
            (r0, u0), (r1, u1) = found
            first = load(r0, u0)
            if u0 % 2:
                first = pltpu.roll(first, HEAD // 2, 1)
            if r0 == r1 and u0 % 2 == 0 and u1 == u0 + 1:
                value = first
            else:
                second = load(r1, u1)
                if u1 % 2 == 0:
                    second = pltpu.roll(second, HEAD // 2, 1)
                value = jnp.where(lower, first, second)
            finish(b, pl.ds(t * HEAD, HEAD), value[:UNIT], value[UNIT:])

    for group, (first, count) in enumerate(GROUPS):
        for k in range(1, SIDE):
            wait_bytes(out_recv.at[pl.ds(first, count), (rank + SIDE - k) % SIDE], res_recv.at[group, k - 1])
        for b in range(first, first + count):
            pl.when(core == 0)(lambda b=b: finish_straight(b))
            pl.when(core == 1)(lambda b=b: finish_crossed(b))

    for j in range(PARTS):
        for half in range(2):
            wait_bytes(xkv.at[j, pl.ds(2 * half, 2), pl.ds(0, NT - 1)], kv_send.at[j, half])
        for group in (None,) if j < LAST else range(len(GROUPS)):
            blocks, i = span(group), slot(j, group)
            wait_bytes(xq.at[j, :, blocks, pl.ds(0, NT - 1)], q_send.at[i])
            wait_bytes(att.at[j, blocks, :, pl.ds(0, NT - 1)], back_send.at[i])
            for k in range(SIDE - 1):
                wait_bytes(tok.at[j, rank, blocks], tok_send.at[i, k])
    for direction in range(2):
        for s in range(5):
            which = ((z + RING - s) if direction == 0 else (z + s)) % RING
            done = lambda which=which, direction=direction, s=s: ring_copy(which, direction, s).wait_send()
            if s < 2:
                done()
            else:
                pl.when(s < reach(which, direction))(done)
    for k in range(7):
        wait_bytes(slab(own_slot, core), w_send.at[k])
    for group, (first, count) in enumerate(GROUPS):
        for k in range(SIDE - 1):
            wait_bytes(out_send.at[pl.ds(first, count), 0], res_send.at[group, k])


def shards(projected, projected_tan, hidden, hidden_tan, out_weight, gate_table, gate_rate, timestep):
    proj = jnp.transpose(projected, (0, 2, 1, 3)).reshape(3, BLOCKS, UNIT, D)
    ptan = jnp.transpose(projected_tan, (0, 2, 1, 3)).reshape(3, BLOCKS, UNIT, D)
    any_spec = pl.BlockSpec(memory_space=pl.ANY)
    vmem = pl.BlockSpec(memory_space=pltpu.VMEM)
    bf16 = jnp.bfloat16
    dma = pltpu.SemaphoreType.DMA
    block_out, block_tan = pl.pallas_call(
        kernel,
        out_shape=(jax.ShapeDtypeStruct((ROWS, D), bf16), jax.ShapeDtypeStruct((ROWS, D), bf16)),
        in_specs=[any_spec] * 7 + [pl.BlockSpec(memory_space=pltpu.SMEM)],
        out_specs=(vmem, vmem),
        scratch_shapes=[
            pltpu.VMEM((PARTS, 4, NT, BLOCKS, UNIT, HEAD), bf16),
            pltpu.VMEM((PARTS, 2, BLOCKS, NT, UNIT, HEAD), bf16),
            pltpu.VMEM((PARTS, BLOCKS, 2, NT, UNIT, HEAD), bf16),
            pltpu.VMEM((PARTS, SIDE, BLOCKS, 2, UNIT, NT * HEAD), bf16),
            pltpu.VMEM((PARTS, SLICE, NT * HEAD), bf16),
            pltpu.VMEM((TILES, SIDE, BLOCKS, 2 * UNIT, TILE), jnp.float32),
            pltpu.VMEM((BLOCKS, SIDE, TILES, 2, UNIT, TILE), bf16),
            pltpu.VMEM((BLOCKS, SIDE, TILES, 2, UNIT, TILE), bf16),
            pltpu.VMEM((ROWS, D), bf16),
            pltpu.VMEM((ROWS, D), bf16),
            pltpu.VMEM((32, D), jnp.float32),
            pltpu.VMEM((32, D), jnp.float32),
            dma((PARTS, 2)),
            dma((PARTS, 2)),
            dma((LAST + len(GROUPS),)),
            dma((LAST + len(GROUPS),)),
            dma((LAST + len(GROUPS),)),
            dma((LAST + len(GROUPS),)),
            dma((LAST + len(GROUPS), SIDE - 1)),
            dma((LAST + len(GROUPS), SIDE - 1)),
            dma((2, 5)),
            dma((2, 5)),
            dma((7,)),
            dma((7,)),
            dma((len(GROUPS), SIDE - 1)),
            dma((len(GROUPS), SIDE - 1)),
            dma((4,)),
            dma((1,)),
        ],
        compiler_params=pltpu.CompilerParams(
            collective_id=0, has_side_effects=True, vmem_limit_bytes=56 * 1024 * 1024
        ),
    )(
        proj,
        ptan,
        hidden.reshape(ROWS, D),
        hidden_tan.reshape(ROWS, D),
        out_weight.T,
        gate_table,
        gate_rate,
        timestep,
    )
    return block_out[None], block_tan[None]


def solution(mesh):
    return jax.shard_map(
        shards,
        mesh=mesh,
        in_specs=(
            P("dp", "tensor", None, None),
            P("dp", "tensor", None, None),
            P("dp", "tensor", None),
            P("dp", "tensor", None),
            P("tensor", "dp"),
            P(),
            P(),
            P("dp"),
        ),
        out_specs=(P("dp", "tensor", None), P("dp", "tensor", None)),
        check_vma=False,
    )
```

time: 166 us -> 155 us (0.934)
  Pallas kernels: 160 us -> 149 us
    pallas_call x1, Pallas kernels: 160 us -> 149 us  [shards(): pl.pallas_call(kernel, out_shape=(jax.ShapeDtypeStruct((ROWS, D), bf16),...]
where the time goes in v3:
time: 155 us
  Pallas kernels  149 us (96%)
  local copies, waits for them, and re-layouts  3.93 us (3%)
    pallas_call x1, Pallas kernels, shards(): pl.pallas_call(kernel, out_shape=(jax.ShapeDtypeStruct((ROWS, D), bf16),...  149 us
    unnamed x2, local copies, waits for them, and re-layouts  3.93 us

profile of v3, /device:TPU:1, one launch (start us, length us, event | category | flops | bytes accessed | tf_op | source)
XLA Modules:
  0.0 154.7 jit_solution(10352524605996526682)
XLA Ops:
  1.3 149.4 %shard_map.95 = (bf16[64,5120]{1,0:T(8,128)(2,1)}, bf16[64,5120]{1,0:T(8,128)(2,1)}) custom-call(bf16[3,4,16,5120]{3,2,1,0:T(8,128)(2,1)} %bitcast.11, bf16[3,4,16,5120]{3,2,1,0:T(8,128)(2,1)} %bitcast.12, bf16[64,5120]{1,0:T(8,128)(2,1)} %bitcast.15, bf16[64,5120]{1,0:T(8,128)(2,1)} %bitcast.16, bf16[160,640]{1,0:T(8,128)(2,1)} %bitcast.17, ...), custom_call_target="tpu_custom_call" | custom-call | tf_op jit(solution)/shard_map/pallas_call | solution.py:450
  150.7 2.0 %copy.13 = bf16[1,64,5120]{2,1,0:T(8,128)(2,1)} copy(bf16[1,64,5120]{2,1,0:T(8,128)(2,1)} %bitcast.14) | data formatting | bytes 1310720
  152.7 2.0 %copy.14 = bf16[1,64,5120]{2,1,0:T(8,128)(2,1)} copy(bf16[1,64,5120]{2,1,0:T(8,128)(2,1)} %bitcast.13) | data formatting | bytes 1310720

commit v4 on v3

--- a/solution.py
+++ b/solution.py
@@ -15,6 +15,7 @@
 UNIT = ROWS // BLOCKS
 ALL = (0, BLOCKS)
 GROUPS = ((0, 2), (2, 2))
+OUT_GROUPS = ((0, 2), (2, 2))
 LAST = 4
 NT = 8
 SIDE = 4
@@ -178,7 +179,7 @@
         i = slot(j, group)
         mine = tok.at[j, rank, span(group)]
         wait_bytes(mine, back_recv.at[i])
-        for k in range(1, SIDE):
+        for k in (2, 1, 3):
             remote(mine, mine, tok_send.at[i, k - 1], tok_recv.at[i, k - 1], row_peer(k))
 
     def wait_tokens(j, group=None):
@@ -230,7 +231,7 @@
         lax.fori_loop(0, TILES, tile, 0)
 
     def project_last(group):
-        first, count = GROUPS[group]
+        first, count = OUT_GROUPS[group]
         rows = tok[LAST, :, first : first + count].reshape(SIDE * count * 2 * UNIT, NT * HEAD)
 
         def tile(n, carry):
@@ -247,7 +248,7 @@
 
         lax.fori_loop(0, TILES, tile, 0)
         blocks = pl.ds(first, count)
-        for k in range(1, SIDE):
+        for k in (2, 1, 3):
             remote(
                 out_send.at[blocks, (rank + k) % SIDE],
                 out_recv.at[blocks, rank],
@@ -327,14 +328,26 @@
             if 2 * j + half < 5:
                 ring_wait(2 * j + half)
             wait_kv(j, half)
-            start_kv(j + 1, half)
+            if j + 1 < LAST or half == 0:
+                start_kv(j + 1, half)
         wait_q(j)
         attend_all(j)
         start_back(j)
+        if j + 1 == LAST:
+            start_kv(LAST, 1)
         if j + 1 < LAST:
             start_q(j + 1)
         if j >= 1:
             start_tokens(j - 1)
+    for copy in residual:
+        copy.wait()
+    level = timestep[0]
+    levels = lax.broadcasted_iota(jnp.int32, gates.shape, 0)
+    gate_row = jnp.sum(jnp.where(levels == level, gates[...], 0.0), axis=0, keepdims=True)
+    rate_row = jnp.sum(jnp.where(levels == level, rates[...], 0.0), axis=0, keepdims=True)
+    gates[0:1, :] = gate_row
+    rates[0:1, :] = rate_row
+
     wait_weights()
     for j in range(2):
         wait_tokens(j)
@@ -351,23 +364,17 @@
         wait_q(LAST, group)
         attend(LAST, *GROUPS[group])
         start_back(LAST, group)
-        if group >= 1:
-            start_tokens(LAST, group - 1)
-    start_tokens(LAST, last - 1)
-    wait_tokens(3)
-    project(3)
     for group in range(last):
-        wait_tokens(LAST, group)
+        start_tokens(LAST, group)
+        if group == 0:
+            wait_tokens(3)
+            project(3)
+    arrived = 0
+    for group, (first, count) in enumerate(OUT_GROUPS):
+        while arrived < last and GROUPS[arrived][0] < first + count:
+            wait_tokens(LAST, arrived)
+            arrived += 1
         project_last(group)
-
-    for copy in residual:
-        copy.wait()
-    level = timestep[0]
-    levels = lax.broadcasted_iota(jnp.int32, gates.shape, 0)
-    gate_row = jnp.sum(jnp.where(levels == level, gates[...], 0.0), axis=0, keepdims=True)
-    rate_row = jnp.sum(jnp.where(levels == level, rates[...], 0.0), axis=0, keepdims=True)
-    gates[0:1, :] = gate_row
-    rates[0:1, :] = rate_row
 
     def finish(b, columns, value, value_tan):
         rows = pl.ds(b * UNIT, UNIT)
@@ -409,7 +416,7 @@
                 value = jnp.where(lower, first, second)
             finish(b, pl.ds(t * HEAD, HEAD), value[:UNIT], value[UNIT:])
 
-    for group, (first, count) in enumerate(GROUPS):
+    for group, (first, count) in enumerate(OUT_GROUPS):
         for k in range(1, SIDE):
             wait_bytes(out_recv.at[pl.ds(first, count), (rank + SIDE - k) % SIDE], res_recv.at[group, k - 1])
         for b in range(first, first + count):
@@ -435,7 +442,7 @@
                 pl.when(s < reach(which, direction))(done)
     for k in range(7):
         wait_bytes(slab(own_slot, core), w_send.at[k])
-    for group, (first, count) in enumerate(GROUPS):
+    for group, (first, count) in enumerate(OUT_GROUPS):
         for k in range(SIDE - 1):
             wait_bytes(out_send.at[pl.ds(first, count), 0], res_send.at[group, k])
 
@@ -477,8 +484,8 @@
             dma((2, 5)),
             dma((7,)),
             dma((7,)),
-            dma((len(GROUPS), SIDE - 1)),
-            dma((len(GROUPS), SIDE - 1)),
+            dma((len(OUT_GROUPS), SIDE - 1)),
+            dma((len(OUT_GROUPS), SIDE - 1)),
             dma((4,)),
             dma((1,)),
         ],

time: 155 us -> 153 us (0.987)
    pallas_call x1, Pallas kernels: 149 us -> 148 us  [shards(): pl.pallas_call(kernel, out_shape=(jax.ShapeDtypeStruct((ROWS, D), bf16),...]
where the time goes in v4:
time: 153 us
  Pallas kernels  148 us (97%)
  local copies, waits for them, and re-layouts  3.93 us (3%)
    pallas_call x1, Pallas kernels, shards(): pl.pallas_call(kernel, out_shape=(jax.ShapeDtypeStruct((ROWS, D), bf16),...  148 us
    unnamed x2, local copies, waits for them, and re-layouts  3.93 us

profile of v4, /device:TPU:1, one launch (start us, length us, event | category | flops | bytes accessed | tf_op | source)
XLA Modules:
  0.0 153.1 jit_solution(3202331156247923035)
XLA Ops:
  1.3 147.8 %shard_map.95 = (bf16[64,5120]{1,0:T(8,128)(2,1)}, bf16[64,5120]{1,0:T(8,128)(2,1)}) custom-call(bf16[3,4,16,5120]{3,2,1,0:T(8,128)(2,1)} %bitcast.11, bf16[3,4,16,5120]{3,2,1,0:T(8,128)(2,1)} %bitcast.12, bf16[64,5120]{1,0:T(8,128)(2,1)} %bitcast.15, bf16[64,5120]{1,0:T(8,128)(2,1)} %bitcast.16, bf16[160,640]{1,0:T(8,128)(2,1)} %bitcast.17, ...), custom_call_target="tpu_custom_call" | custom-call | tf_op jit(solution)/shard_map/pallas_call | solution.py:457
  149.1 2.0 %copy.13 = bf16[1,64,5120]{2,1,0:T(8,128)(2,1)} copy(bf16[1,64,5120]{2,1,0:T(8,128)(2,1)} %bitcast.14) | data formatting | bytes 1310720
  151.1 2.0 %copy.14 = bf16[1,64,5120]{2,1,0:T(8,128)(2,1)} copy(bf16[1,64,5120]{2,1,0:T(8,128)(2,1)} %bitcast.13) | data formatting | bytes 1310720

commit v5 on v4

--- a/solution.py
+++ b/solution.py
@@ -41,9 +41,9 @@
 
 
 def kernel(
-    proj, ptan, hidden, hidden_tan, weight, gate_table, gate_rate, timestep,
-    out, out_tan,
-    xkv, xq, att, tok, wbuf, acc, out_send, out_recv, hid, hid_tan, gates, rates,
+    proj, ptan, weight, gate_table, gate_rate, timestep,
+    change,
+    xkv, xq, att, tok, wbuf, acc, out_send, out_recv, gates, rates,
     kv_send, kv_recv, q_send, q_recv, back_send, back_recv, tok_send, tok_recv,
     z_send, z_recv, w_send, w_recv, res_send, res_recv, local_sem, own_sem,
 ):
@@ -101,7 +101,7 @@
     residual = [
         pltpu.make_async_copy(source, target, local_sem.at[i])
         for i, (source, target) in enumerate(
-            ((hidden, hid), (hidden_tan, hid_tan), (gate_table, gates), (gate_rate, rates))
+            ((gate_table, gates), (gate_rate, rates))
         )
     ]
     for copy in residual:
@@ -379,10 +379,8 @@
     def finish(b, columns, value, value_tan):
         rows = pl.ds(b * UNIT, UNIT)
         gate, rate = gates[0:1, columns], rates[0:1, columns]
-        out[rows, columns] = (hid[rows, columns].astype(jnp.float32) + gate * value).astype(jnp.bfloat16)
-        out_tan[rows, columns] = (
-            hid_tan[rows, columns].astype(jnp.float32) + gate * value_tan + rate * value
-        ).astype(jnp.bfloat16)
+        change[0, rows, columns] = gate * value
+        change[1, rows, columns] = gate * value_tan + rate * value
 
     def finish_straight(b):
         for r in range(SIDE):
@@ -454,11 +452,11 @@
     vmem = pl.BlockSpec(memory_space=pltpu.VMEM)
     bf16 = jnp.bfloat16
     dma = pltpu.SemaphoreType.DMA
-    block_out, block_tan = pl.pallas_call(
+    change = pl.pallas_call(
         kernel,
-        out_shape=(jax.ShapeDtypeStruct((ROWS, D), bf16), jax.ShapeDtypeStruct((ROWS, D), bf16)),
-        in_specs=[any_spec] * 7 + [pl.BlockSpec(memory_space=pltpu.SMEM)],
-        out_specs=(vmem, vmem),
+        out_shape=jax.ShapeDtypeStruct((2, ROWS, D), jnp.float32),
+        in_specs=[any_spec] * 5 + [pl.BlockSpec(memory_space=pltpu.SMEM)],
+        out_specs=vmem,
         scratch_shapes=[
             pltpu.VMEM((PARTS, 4, NT, BLOCKS, UNIT, HEAD), bf16),
             pltpu.VMEM((PARTS, 2, BLOCKS, NT, UNIT, HEAD), bf16),
@@ -468,8 +466,6 @@
             pltpu.VMEM((TILES, SIDE, BLOCKS, 2 * UNIT, TILE), jnp.float32),
             pltpu.VMEM((BLOCKS, SIDE, TILES, 2, UNIT, TILE), bf16),
             pltpu.VMEM((BLOCKS, SIDE, TILES, 2, UNIT, TILE), bf16),
-            pltpu.VMEM((ROWS, D), bf16),
-            pltpu.VMEM((ROWS, D), bf16),
             pltpu.VMEM((32, D), jnp.float32),
             pltpu.VMEM((32, D), jnp.float32),
             dma((PARTS, 2)),
@@ -486,7 +482,7 @@
             dma((7,)),
             dma((len(OUT_GROUPS), SIDE - 1)),
             dma((len(OUT_GROUPS), SIDE - 1)),
-            dma((4,)),
+            dma((2,)),
             dma((1,)),
         ],
         compiler_params=pltpu.CompilerParams(
@@ -495,14 +491,14 @@
     )(
         proj,
         ptan,
-        hidden.reshape(ROWS, D),
-        hidden_tan.reshape(ROWS, D),
         out_weight.T,
         gate_table,
         gate_rate,
         timestep,
     )
-    return block_out[None], block_tan[None]
+    block_out = (hidden.astype(jnp.float32) + change[:1]).astype(bf16)
+    block_tan = (hidden_tan.astype(jnp.float32) + change[1:]).astype(bf16)
+    return block_out, block_tan
 
 
 def solution(mesh):

time: 153 us -> 153 us (level)
  local copies, waits for them, and re-layouts: 3.93 us -> 0.01 us
  other arithmetic: 0 us -> 3.02 us
    unnamed x2 -> x4, local copies, waits for them, and re-layouts: 3.93 us -> 0.01 us
    convert_element_type x0 -> x1, other arithmetic: none -> 3.02 us  [shards(): block_tan = (hidden_tan.astype(jnp.float32) + change[1:]).astype(bf16)]
where the time goes in v5:
time: 153 us; the launch traced here: 152 us
  Pallas kernels  148 us (97%)
  other arithmetic  3.02 us (2%)
    pallas_call x1, Pallas kernels, shards(): pl.pallas_call(kernel, out_shape=jax.ShapeDtypeStruct((2, ROWS, D), jnp.f...  148 us

profile of v5, /device:TPU:1, one launch (start us, length us, event | category | flops | bytes accessed | tf_op | source)
XLA Modules:
  0.0 152.5 jit_solution(18231072037307664373)
XLA Ops:
  1.3 0.0 copy-start
  1.3 0.0 copy-start.1
  1.3 148.1 %shard_map.95 = f32[2,64,5120]{2,1,0:T(8,128)} custom-call(bf16[3,4,16,5120]{3,2,1,0:T(8,128)(2,1)} %bitcast.7, bf16[3,4,16,5120]{3,2,1,0:T(8,128)(2,1)} %bitcast.8, bf16[160,640]{1,0:T(8,128)(2,1)} %bitcast.9, f32[32,5120]{1,0:T(8,128)} %gate_table.1, f32[32,5120]{1,0:T(8,128)} %gate_rate.1, s32[1]{0:T(128)S(6)} %copy.10.timestep), custom_call_target="tpu_custom_call" | custom-call | tf_op jit(solution)/shard_map/pallas_call | solution.py:455
  149.4 0.0 copy-done
  149.5 0.0 copy-done.1
  149.5 3.0 %add_convert_fusion = (bf16[1,64,5120]{2,1,0:T(8,128)(2,1)}, bf16[1,64,5120]{2,1,0:T(8,128)(2,1)}) fusion(f32[2,64,5120]{2,1,0:T(8,128)} %shard_map.95, bf16[1,64,5120]{2,1,0:T(8,128)(2,1)S(1)} %copy-done, bf16[1,64,5120]{2,1,0:T(8,128)(2,1)S(1)} %copy-done.1), kind=kLoop, calls=%fused_computation | loop fusion | flops 1966080 | bytes 5242880 | tf_op jit(solution)/shard_map/convert_element_type | solution.py:500
Async XLA Ops:
  1.3 148.2 %copy-start = (bf16[1,64,5120]{2,1,0:T(8,128)(2,1)S(1)}, bf16[1,64,5120]{2,1,0:T(8,128)(2,1)}, u32[]{:S(2)}) copy-start(bf16[1,64,5120]{2,1,0:T(8,128)(2,1)} %param.11) | copy-start | bytes 1966084
  1.3 148.2 %copy-start.1 = (bf16[1,64,5120]{2,1,0:T(8,128)(2,1)S(1)}, bf16[1,64,5120]{2,1,0:T(8,128)(2,1)}, u32[]{:S(2)}) copy-start(bf16[1,64,5120]{2,1,0:T(8,128)(2,1)} %param.10) | copy-start | bytes 1966084
